TPU v7x, 32 devices: a whole 2x2x4 slice. The times are simulated.
32 devices in a mesh: ens: 2 (over y), tile: 4 (over z), chan: 2 (over x), sec: 2 (over core).
Axes of the slice: x: 2, y: 2, z: 4, core: 2. Of those that a mesh axis runs over, the one named last changes fastest.
Arguments:
- ocean_state: bfloat16 [256, 128, 4, 128], P(('chan', 'sec'), ('ens', 'tile')), parts along dimension 1, may hold values from -6 to 6
- atmos: bfloat16 [16384, 384], P(('ens', 'tile')), parts along dimension 0, may hold values from -6 to 6
- flux_weight: bfloat16 [384, 256], P(None, ('chan', 'sec')), may hold values from -0.3125 to 0.3125
- conv_weight: bfloat16 [9, 256, 256], P(None, None, ('chan', 'sec')), may hold values from -0.125 to 0.125
- conv_bias: bfloat16 [256], P(('chan', 'sec')), may hold values from -3 to 3
- norm_gain: bfloat16 [256], P(('chan', 'sec')), may hold values from 0.5 to 2
- in_weight: bfloat16 [256, 1024], P(None, ('chan', 'sec')), may hold values from -0.375 to 0.375
- in_bias: bfloat16 [1024], P(('chan', 'sec')), may hold values from -3 to 3
- out_weight: bfloat16 [1024, 256], P(('chan', 'sec')), may hold values from -0.25 to 0.25
- layer_scale: bfloat16 [256], P(('chan', 'sec')), may hold values from 0.5 to 2
- cell_mask: int32 [64, 4, 128], P('tile'), may hold values from 0 to 1, as said below
- neighbours: int32 [64, 8], P('tile'), may hold values from -1 to 63, as said below
- remap: int32 [64, 4, 128], P('tile'), may hold values from 0 to 8191
Outputs:
- ocean_next: bfloat16 [256, 128, 4, 128], P(('chan', 'sec'), ('ens', 'tile')), parts along dimension 1
There are 2 independent parts, one for each index of `ens`. A program takes and returns all parts, laid end to end along the dimension named above; an argument that names none is the same for every part. Nothing has to cross between parts.
Inputs may be any that keep to these rules, and one draw needn't show every extreme that they name: `cell_mask`: land cells and every cell of a land block are 0. `neighbours`: for a slot among those of tile index t, each entry is -1 or a slot among those of tile indices t - 1, t and t + 1, i.e. in [(t - 1) * 16, (t + 2) * 16); entries that name land blocks are -1.
All inputs are finite; a program needn't handle non-finite values.
Results may differ from a plain program's by a relative error of at most 0.01.
Values may be sent and summed in bfloat16 or wider, within the bound.
A program may use at most 64 MiB of HBM per device.

v0:
```python
import jax
import jax.numpy as jnp
from jax import lax
from jax.sharding import PartitionSpec as P

norm_eps = 1e-06


def padded_2(cells, sides, width):
    for axis, dim in sides:
        count = lax.axis_size(axis)
        ends = count - 1
        head = lax.slice_in_dim(cells, 0, width, axis=dim)
        tail = lax.slice_in_dim(cells, cells.shape[dim] - width, cells.shape[dim], axis=dim)
        cells = jnp.concatenate(
            [
                lax.ppermute(tail, axis, [(i, (i + 1) % count) for i in range(ends)]),
                cells,
                lax.ppermute(head, axis, [((i + 1) % count, i) for i in range(ends)]),
            ],
            axis=dim,
        )
    return cells


def strips_of(state):
    return jnp.concatenate(
        [
            state[:, :, 0, :],
            state[:, :, -1, :],
            state[:, :, :, 0],
            state[:, :, :, -1],
            state[:, :, 0, 0:1],
            state[:, :, 0, -1:],
            state[:, :, -1, 0:1],
            state[:, :, -1, -1:],
        ],
        axis=2,
    )


def pad_blocks(state, strips, slot_index, valid):
    channels, slot_count, block_rows, block_cols = state.shape
    width = strips.shape[2]
    picked = jnp.take(strips, slot_index.reshape(-1), axis=1).reshape(
        channels, slot_count, 8, width
    )
    picked = jnp.where(valid[None, :, :, None], picked, jnp.zeros_like(picked))
    offset_base = 2 * block_cols + 2 * block_rows
    west_col = picked[:, :, 0, 2 * block_cols + block_rows : offset_base]
    east_col = picked[:, :, 1, 2 * block_cols : 2 * block_cols + block_rows]
    prev_row = picked[:, :, 2, block_cols : 2 * block_cols]
    next_row = picked[:, :, 3, 0:block_cols]
    top_row = jnp.concatenate(
        [
            picked[:, :, 4, offset_base + 3 : offset_base + 4],
            prev_row,
            picked[:, :, 5, offset_base + 2 : offset_base + 3],
        ],
        axis=2,
    )
    bottom_row = jnp.concatenate(
        [
            picked[:, :, 6, offset_base + 1 : offset_base + 2],
            next_row,
            picked[:, :, 7, offset_base : offset_base + 1],
        ],
        axis=2,
    )
    middle = jnp.concatenate([west_col[:, :, :, None], state, east_col[:, :, :, None]], axis=3)
    return jnp.concatenate([top_row[:, :, None, :], middle, bottom_row[:, :, None, :]], axis=2)


def conv_taps(padded, kernel, block_rows, block_cols):
    total = jnp.zeros((kernel.shape[2], padded.shape[1], block_rows, block_cols), jnp.float32)
    for tap in range(9):
        tap_row = tap // 3
        tap_col = tap % 3
        window = padded[:, :, tap_row : tap_row + block_rows, tap_col : tap_col + block_cols]
        total = total + jnp.einsum(
            "cskl,co->oskl", window, kernel[tap], preferred_element_type=jnp.float32
        )
    return total


def add_group(total, pair):
    term = jnp.einsum("hsij,hc->csij", pair[0], pair[1], preferred_element_type=jnp.float32).astype(
        jnp.bfloat16
    )
    term = lax.optimization_barrier(term)
    return (total + term.astype(jnp.float32), None)


def on_device(
    ocean_state,
    atmos,
    flux_weight,
    conv_weight,
    conv_bias,
    norm_gain,
    in_weight,
    in_bias,
    out_weight,
    layer_scale,
    cell_mask,
    neighbours,
    remap,
):
    chan_local, slot_count, block_rows, block_cols = ocean_state.shape
    groups = lax.axis_size(("chan", "sec"))
    channels = chan_local * groups
    hid_local = in_weight.shape[1]
    extended = padded_2(strips_of(ocean_state), (("tile", 1),), slot_count)
    first_slot = (lax.axis_index("tile") - 1) * slot_count
    valid = neighbours >= 0
    slot_index = jnp.clip(neighbours - first_slot, 0, 3 * slot_count - 1)
    padded = pad_blocks(ocean_state, extended, slot_index, valid)
    local_flux = jnp.einsum(
        "rf,fc->cr", atmos, flux_weight, preferred_element_type=jnp.float32
    ).astype(jnp.bfloat16)
    targets = remap.reshape(-1)
    piece = lax.all_gather(local_flux, "tile", axis=1, tiled=True)
    inside = (targets >= 0) & (targets < piece.shape[1])
    values = jnp.take(piece, jnp.clip(targets, 0, piece.shape[1] - 1), axis=1)
    forcing = jnp.where(inside[None, :], values, jnp.zeros_like(values))
    full_kernel, full_bias, full_gain, full_in, full_in_bias, full_out = (
        lax.all_gather(conv_weight, ("chan", "sec"), axis=2, tiled=True),
        lax.all_gather(conv_bias, ("chan", "sec"), axis=0, tiled=True),
        lax.all_gather(norm_gain, ("chan", "sec"), axis=0, tiled=True),
        lax.all_gather(in_weight, ("chan", "sec"), axis=1, tiled=True),
        lax.all_gather(in_bias, ("chan", "sec"), axis=0, tiled=True),
        lax.all_gather(out_weight, ("chan", "sec"), axis=0, tiled=True),
    )
    out_groups = full_out.reshape(groups, hid_local, channels)
    grouped = padded.reshape(
        chan_local, groups, slot_count // groups, block_rows + 2, block_cols + 2
    )
    tiles = lax.all_to_all(grouped, ("chan", "sec"), split_axis=1, concat_axis=0, tiled=True)[:, 0]
    conv_out = (
        conv_taps(tiles, full_kernel, block_rows, block_cols)
        + full_bias.astype(jnp.float32)[:, None, None, None]
    )
    squares = jnp.sum(conv_out * conv_out, axis=0)
    normed = (
        conv_out
        * lax.rsqrt(squares / channels + norm_eps)
        * full_gain.astype(jnp.float32)[:, None, None, None]
    ).astype(jnp.bfloat16)
    pre = jnp.einsum("csij,ch->hsij", normed, full_in, preferred_element_type=jnp.float32)
    hidden = jax.nn.gelu(
        pre + full_in_bias.astype(jnp.float32)[:, None, None, None], approximate=False
    ).astype(jnp.bfloat16)
    hid_groups = hidden.reshape((groups, hid_local) + hidden.shape[1:])
    summed, _ = lax.scan(
        add_group, jnp.zeros((channels,) + hidden.shape[1:], jnp.float32), (hid_groups, out_groups)
    )
    update = lax.all_to_all(
        summed[:, None], ("chan", "sec"), split_axis=0, concat_axis=1, tiled=True
    )
    update = update.reshape(chan_local, slot_count, block_rows, block_cols)
    total = (
        ocean_state.astype(jnp.float32)
        + layer_scale.astype(jnp.float32)[:, None, None, None] * update
    )
    total = total + forcing.reshape(chan_local, slot_count, block_rows, block_cols).astype(
        jnp.float32
    )
    return (cell_mask.astype(jnp.float32)[None] * total).astype(jnp.bfloat16)


def solution(mesh):
    placed = (
        P(("chan", "sec"), ("ens", "tile"), None, None),
        P(("ens", "tile"), None),
        P(None, ("chan", "sec")),
        P(None, None, ("chan", "sec")),
        P(("chan", "sec")),
        P(("chan", "sec")),
        P(None, ("chan", "sec")),
        P(("chan", "sec")),
        P(("chan", "sec"), None),
        P(("chan", "sec")),
        P("tile", None, None),
        P("tile", None),
        P("tile", None, None),
    )
    return jax.shard_map(
        on_device,
        mesh=mesh,
        in_specs=placed,
        out_specs=P(("chan", "sec"), ("ens", "tile"), None, None),
        check_vma=False,
    )
```

profile of v0, /device:TPU:0, one launch (start us, length us, event | category | flops | bytes accessed | tf_op | source)
XLA Modules:
  0.0 303.2 jit_solution(8548367868448448992)
XLA Ops:
  6.5 3.6 %fusion.51 = (bf16[64,16,1,128]{3,2,1,0:T(2,128)(2,1)S(1)}, bf16[64,16,1,128]{3,2,1,0:T(2,128)(2,1)}) fusion(bf16[64,16,4,128]{3,2,1,0:T(4,128)(2,1)} %param.15), kind=kLoop, calls=%fused_computation.95 | loop fusion | bytes 1048576 | tf_op jit(solution)/shard_map/slice | solution.py:30
  10.2 3.0 fusion.49
  13.2 2.3 fusion.50
  15.5 1.3 copy.122
  22.1 1.3 copy.125
  24.3 7.2 %copy.136 = bf16[64,16,4,1]{2,0,1,3:T(8,128)(2,1)S(1)} copy(bf16[64,16,4,1]{3,2,1,0:T(4,128)(2,1)} %get-tuple-element.80) | data formatting | bytes 16384 | tf_op jit(solution)/shard_map/squeeze | solution.py:31
  31.6 7.9 %copy.137 = bf16[64,16,4,1]{2,0,1,3:T(8,128)(2,1)} copy(bf16[64,16,4,1]{3,2,1,0:T(4,128)(2,1)} %get-tuple-element.79) | data formatting | bytes 16384 | tf_op jit(solution)/shard_map/squeeze | solution.py:32
  39.5 2.2 copy_bitcast_fusion.1
  41.6 3.6 %concatenate.40 = bf16[64,16,268]{2,0,1:T(8,128)(2,1)} concatenate(bf16[64,16,128]{2,0,1:T(8,128)(2,1)} %get-tuple-element.89, bf16[64,16,128]{2,0,1:T(8,128)(2,1)} %get-tuple-element.88, bf16[64,16,4]{2,0,1:T(8,128)(2,1)S(1)} %bitcast.225, bf16[64,16,4]{2,0,1:T(8,128)(2,1)} %bitcast.226, bf16[64,16,1]{2,0,1:T(8,128)(2,1)} %copy.73, bf16[64,16,1]{2,0,1:T(8,128)(2,1)} %copy.74, ...), dimensions={2} | concatenate | bytes 1097728 | tf_op jit(solution)/shard_map/concatenate | solution.py:27
  45.3 5.8 %collective-permute-start = (bf16[64,16,268]{2,0,1:T(8,128)(2,1)}, bf16[64,16,268]{2,0,1:T(8,128)(2,1)}, u32[]{:S(2)}, u32[]{:S(2)}) collective-permute-start(bf16[64,16,268]{2,0,1:T(8,128)(2,1)} %concatenate.40), channel_id=1, source_target_pairs={{0,4},{4,8},{8,12},{1,5},{5,9},{9,13},{2,6},{6,10},{10,14},{3,7},{... | collective-permute-start | bytes 1646600 | tf_op jit(solution)/shard_map/ppermute | solution.py:17
  51.1 1.5 collective-permute-start.1
  52.6 1.6 copy.82
  54.4 12.9 %collective-permute-done = bf16[64,16,268]{2,0,1:T(8,128)(2,1)} collective-permute-done((bf16[64,16,268]{2,0,1:T(8,128)(2,1)}, bf16[64,16,268]{2,0,1:T(8,128)(2,1)}, u32[]{:S(2)}, u32[]{:S(2)}) %collective-permute-start) | collective-permute-done | bytes 548896 | tf_op jit(solution)/shard_map/ppermute | solution.py:17
  67.3 5.0 %collective-permute-done.1 = bf16[64,16,268]{2,0,1:T(8,128)(2,1)} collective-permute-done((bf16[64,16,268]{2,0,1:T(8,128)(2,1)}, bf16[64,16,268]{2,0,1:T(8,128)(2,1)}, u32[]{:S(2)}, u32[]{:S(2)}) %collective-permute-start.1) | collective-permute-done | bytes 548896 | tf_op jit(solution)/shard_map/ppermute | solution.py:19
  72.3 3.5 %pad_maximum_fusion.1 = bf16[64,48,268]{2,0,1:T(8,128)(2,1)} fusion(bf16[64,16,268]{2,0,1:T(8,128)(2,1)} %collective-permute-done.1, bf16[64,16,268]{2,0,1:T(8,128)(2,1)} %concatenate.40, bf16[64,16,268]{2,0,1:T(8,128)(2,1)} %collective-permute-done), kind=kLoop, calls=%fused_computation.35 | loop fusion | flops 1646592 | bytes 3293184 | tf_op jit(solution)/shard_map/concatenate | solution.py:15
  75.8 5.8 %gather_fusion = bf16[128,64,268]{2,1,0:T(8,128)(2,1)} fusion(bf16[64,48,268]{2,0,1:T(8,128)(2,1)} %pad_maximum_fusion.1, s32[1024]{0:T(1024)S(1)} %pad_clamp_fusion), kind=kCustom, calls=%fused_computation | custom fusion | bytes 8782336 | tf_op jit(solution)/shard_map/jit(_take)/gather | solution.py:45
  81.5 13.8 %copy.78 = bf16[64,16,8,268]{0,1,3,2:T(8,128)(2,1)} copy(bf16[64,16,8,268]{3,0,2,1:T(8,128)(2,1)} %bitcast.217) | data formatting | bytes 8781824 | tf_op jit(solution)/shard_map/jit(_take)/gather | solution.py:45
  95.3 7.9 %select_select_fusion = bf16[64,16,8,268]{0,1,3,2:T(8,128)(2,1)} fusion(bf16[64,16,8,268]{0,1,3,2:T(8,128)(2,1)} %copy.78, pred[16,8]{0,1:T(8,128)(4,1)S(1)} %get-tuple-element.65, pred[16,8]{0,1:T(8,128)(4,1)S(1)} %get-tuple-element.85), kind=kLoop, calls=%fused_computation.10 | loop fusion | flops 4390912 | bytes 8782080 | tf_op jit(solution)/shard_map/jit(_where)/select_n | solution.py:48
  105.8 1.4 fusion.47
  111.3 1.5 copy.83
  112.8 1.4 copy.84
  114.2 1.5 maximum_bitcast_fusion
  115.7 1.4 maximum_bitcast_fusion.1
  117.2 3.0 pad_maximum_fusion
  120.3 4.8 %all-to-all-start = ((bf16[64,4,4,6,130]{4,0,3,2,1:T(8,128)(2,1)}), bf16[64,4,4,6,130]{4,0,3,2,1:T(8,128)(2,1)}, u32[]{:S(2)}, u32[]{:S(2)}) async-start(bf16[64,4,4,6,130]{4,0,3,2,1:T(8,128)(2,1)} %pad_maximum_fusion), calls=%async_computation | async-start | bytes 6291456 | tf_op jit(solution)/shard_map/all_to_all | solution.py:138
  125.1 1.3 convolution_convert_fusion.1
  128.3 35.2 %all-reduce.2 = (bf16[256]{0:T(256)(128)(2,1)S(1)}, bf16[256]{0:T(256)(128)(2,1)S(1)}) all-reduce(bf16[256]{0:T(256)(128)(2,1)S(1)} %dynamic-update-slice, bf16[256]{0:T(256)(128)(2,1)S(1)} %dynamic-update-slice.1), channel_id=1, replica_groups=mesh['ens'=2,'tile'=4,'chan'=2,'sec'=2] {'chan','sec'}, use_global_device_ids=true, to_apply=%add | all-reduce | flops 512 | bytes 2048
  163.5 5.1 %all-gather = bf16[4,1,256]{2,1,0:T(2,128)(2,1)S(1)} all-gather(bf16[1,1,256]{2,1,0:T(2,128)(2,1)S(1)} %reshape.159), channel_id=1, replica_groups=mesh['ens'=2,'tile'=4,'chan'=2,'sec'=2] {'chan','sec'}, dimensions={0}, use_global_device_ids=true | all-gather | bytes 2560 | tf_op jit(solution)/shard_map/all_gather | solution.py:131
  168.6 7.3 %all_gather.25 = bf16[256,1024]{1,0:T(8,128)(2,1)S(1)} all-gather(bf16[256,256]{1,0:T(8,128)(2,1)S(1)} %copy-done.10), channel_id=1, replica_groups=mesh['ens'=2,'tile'=4,'chan'=2,'sec'=2] {'chan','sec'}, dimensions={1}, use_global_device_ids=true | all-gather | bytes 655360 | tf_op jit(solution)/shard_map/all_gather | solution.py:130
  176.0 7.9 %all_gather.21 = bf16[1024,256]{1,0:T(8,128)(2,1)} all-gather(bf16[256,256]{1,0:T(8,128)(2,1)S(1)} %copy-done.11), channel_id=1, replica_groups=mesh['ens'=2,'tile'=4,'chan'=2,'sec'=2] {'chan','sec'}, dimensions={0}, use_global_device_ids=true | all-gather | bytes 655360 | tf_op jit(solution)/shard_map/all_gather | solution.py:132
  184.0 7.3 %copy.90 = bf16[4,64,1,4,6,130]{1,0,5,4,3,2:T(4,128)(2,1)} copy(bf16[4,64,1,4,6,130]{5,1,4,3,0,2:T(8,128)(2,1)} %bitcast.24) | data formatting | bytes 3194880 | tf_op jit(solution)/shard_map/all_to_all | solution.py:138
  191.3 5.1 %squeeze.76 = bf16[256,4,6,130]{0,3,2,1:T(8,128)(2,1)} reshape(bf16[4,64,1,4,6,130]{1,0,5,4,3,2:T(4,128)(2,1)} %copy.90) | data formatting | bytes 3194880 | tf_op jit(solution)/shard_map/squeeze | solution.py:138
  196.4 1.8 fusion.28
  203.1 20.7 %fusion.7 = bf16[1024,4,4,128]{0,3,2,1:T(8,128)(2,1)} fusion(f32[1024]{0:T(1024)S(1)} %bitcast.239, f32[4,4,128,256]{3,2,1,0:T(8,128)S(1)} %get-tuple-element.87, f32[256]{0:T(256)S(1)} %convert_element_type.43, f32[4,4,128]{2,1,0:T(4,128)S(1)} %add_rsqrt_fusion, bf16[256,1024]{1,0:T(8,128)(2,1)S(1)} %all_gather.25), kind=kOutput, calls=%fused_computation.13 | convolution fusion | flops 1213726720 | bytes 6829056 | tf_op jit(solution)/shard_map/csij,ch->hsij/dot_general | solution.py:149
  223.9 7.9 %reshape.135 = bf16[4,256,4,4,128]{1,0,4,3,2:T(4,128)(2,1)} reshape(bf16[1024,4,4,128]{0,3,2,1:T(8,128)(2,1)} %fusion.7) | data formatting | bytes 8388608 | tf_op jit(solution)/shard_map/reshape | solution.py:153
  231.8 7.5 %copy.101 = bf16[4,256,4,4,128]{4,1,3,2,0:T(8,128)(2,1)} copy(bf16[4,256,4,4,128]{1,0,4,3,2:T(4,128)(2,1)} %reshape.135) | data formatting | bytes 8388608
  239.3 9.9 %while.11 = (s32[]{:T(128)}, f32[256,4,4,128]{3,0,2,1:T(8,128)S(1)}, bf16[4,256,256]{2,1,0:T(8,128)(2,1)}, bf16[4,256,4,4,128]{4,1,3,2,0:T(8,128)(2,1)}, s32[]{:T(128)}, /*index=5*/s32[]{:T(128)}) while((s32[]{:T(128)}, f32[256,4,4,128]{3,0,2,1:T(8,128)S(1)}, bf16[4,256,256]{2,1,0:T(8,128)(2,1)}, ...), condition=%wide.region_2.3_spmd.clone, body=%wide.region_1.2_spmd.clone.sunk | while | flops 270532608 | bytes 7472207 | solution.py:154
  239.3 1.8 convolution_convert_fusion.3
  241.7 1.8 convolution_convert_fusion.3
  244.2 1.8 convolution_convert_fusion.3
  246.7 1.8 convolution_convert_fusion.3
  249.2 2.7 copy.141
  251.8 4.7 %all-to-all-start.1 = ((f32[256,1,4,4,128]{4,3,2,1,0:T(4,128)}), f32[256,1,4,4,128]{4,3,2,1,0:T(4,128)}, u32[]{:S(2)}, u32[]{:S(2)}) async-start(f32[256,1,4,4,128]{4,3,2,1,0:T(4,128)} %bitcast.218), calls=%async_computation.1 | async-start | bytes 4194304 | tf_op jit(solution)/shard_map/all_to_all | solution.py:157
  256.6 2.0 copy.104
  258.7 29.2 %gather_fusion.1 = bf16[8192,64]{1,0:T(8,128)(2,1)} fusion(bf16[64,8192]{0,1:T(8,128)(2,1)S(1)} %copy.104, s32[8192]{0:T(1024)S(1)} %broadcast_clamp_fusion), kind=kCustom, calls=%fused_computation.1 | custom fusion | bytes 2129920 | tf_op jit(solution)/shard_map/jit(_take)/gather | solution.py:124
  287.9 3.7 %copy.105 = bf16[64,16,4,128]{3,2,1,0:T(4,128)(2,1)} copy(bf16[64,16,4,128]{0,3,2,1:T(8,128)(2,1)} %bitcast.220) | data formatting | bytes 2097152 | tf_op jit(solution)/shard_map/jit(_take)/gather | solution.py:124
  291.6 2.3 copy.103
  294.0 2.4 multiply_convert_fusion.1
  (98 shorter events, 22.1 us)
Async XLA Ops:
  6.5 118.6 %copy-start = (bf16[2048,384]{1,0:T(8,128)(2,1)S(1)}, bf16[2048,384]{1,0:T(8,128)(2,1)}, u32[]{:S(2)}) copy-start(bf16[2048,384]{1,0:T(8,128)(2,1)} %param.16) | copy-start | bytes 4718596
  6.5 3.6 %copy-start.3 = (bf16[64,16,4,128]{3,2,1,0:T(4,128)(2,1)S(1)}, bf16[64,16,4,128]{3,2,1,0:T(4,128)(2,1)}, u32[]{:S(2)}) copy-start(bf16[64,16,4,128]{3,2,1,0:T(4,128)(2,1)} %param.15) | copy-start | bytes 3145732
  6.5 189.8 %all-gather.4.cloned.1.call-start = ((), (), s32[]{:S(2)}) async-start(), calls=%async_computation.2 | async-start | bytes 1474560 | tf_op jit(solution)/shard_map/all_gather | solution.py:127
  39.5 14.8 %copy-start.15 = (s32[16,8]{0,1:T(8,128)S(1)}, s32[16,8]{0,1:T(8,128)}, u32[]{:S(2)}) copy-start(s32[16,8]{0,1:T(8,128)} %param.26) | copy-start | bytes 1540
  45.3 22.0 %collective-permute-start = (bf16[64,16,268]{2,0,1:T(8,128)(2,1)}, bf16[64,16,268]{2,0,1:T(8,128)(2,1)}, u32[]{:S(2)}, u32[]{:S(2)}) collective-permute-start(bf16[64,16,268]{2,0,1:T(8,128)(2,1)} %concatenate.40), channel_id=1, source_target_pairs={{0,4},{4,8},{8,12},{1,5},{5,9},{9,13},{2,6},{6,10},{10,14},{3,7},{... | collective-permute-start | bytes 1646600 | tf_op jit(solution)/shard_map/ppermute | solution.py:17
  51.1 21.2 %collective-permute-start.1 = (bf16[64,16,268]{2,0,1:T(8,128)(2,1)}, bf16[64,16,268]{2,0,1:T(8,128)(2,1)}, u32[]{:S(2)}, u32[]{:S(2)}) collective-permute-start(bf16[64,16,268]{2,0,1:T(8,128)(2,1)} %concatenate.40), channel_id=1, source_target_pairs={{4,0},{8,4},{12,8},{5,1},{9,5},{13,9},{6,2},{10,6},{14,10},{7,3},{... | collective-permute-start | bytes 1646600 | tf_op jit(solution)/shard_map/ppermute | solution.py:19
  107.6 9.6 %copy-start.5 = (bf16[64,16,4,128]{3,0,2,1:T(8,128)(2,1)S(1)}, bf16[64,16,4,128]{3,0,2,1:T(8,128)(2,1)}, u32[]{:S(2)}) copy-start(bf16[64,16,4,128]{3,0,2,1:T(8,128)(2,1)} %copy.82) | copy-start | bytes 3145732
  114.2 2.9 copy-start.6
  114.2 2.9 copy-start.7
  120.2 4.9 %copy-start.13 = (bf16[384,64]{0,1:T(8,128)(2,1)S(1)}, bf16[384,64]{0,1:T(8,128)(2,1)}, u32[]{:S(2)}) copy-start(bf16[384,64]{0,1:T(8,128)(2,1)} %param.17) | copy-start | bytes 147460
  120.2 6.3 %copy-start.20 = (u32[32]{0:T(128)S(1)}, u32[32]{0:T(128)}, u32[]{:S(2)}) copy-start(u32[32]{0:T(128)} %constant.127) | copy-start | bytes 388
  120.2 7.6 %copy-start.16 = (bf16[64]{0:T(256)(128)(2,1)S(1)}, bf16[64]{0:T(256)(128)(2,1)}, u32[]{:S(2)}) copy-start(bf16[64]{0:T(256)(128)(2,1)} %param.19) | copy-start | bytes 388
  120.2 7.8 %copy-start.17 = (bf16[64]{0:T(256)(128)(2,1)S(1)}, bf16[64]{0:T(256)(128)(2,1)}, u32[]{:S(2)}) copy-start(bf16[64]{0:T(256)(128)(2,1)} %param.20) | copy-start | bytes 388
  120.2 43.3 %copy-start.18 = (bf16[256]{0:T(256)(128)(2,1)S(1)}, bf16[256]{0:T(256)(128)(2,1)}, u32[]{:S(2)}) copy-start(bf16[256]{0:T(256)(128)(2,1)} %param.22) | copy-start | bytes 1540
  120.2 48.4 %copy-start.14 = (s32[16,4,128]{2,1,0:T(4,128)S(1)}, s32[16,4,128]{2,1,0:T(4,128)}, u32[]{:S(2)}) copy-start(s32[16,4,128]{2,1,0:T(4,128)} %param.25) | copy-start | bytes 98308
  120.2 48.4 %copy-start.19 = (bf16[64]{0:T(256)(128)(2,1)S(1)}, bf16[64]{0:T(256)(128)(2,1)}, u32[]{:S(2)}) copy-start(bf16[64]{0:T(256)(128)(2,1)} %param.24) | copy-start | bytes 388
  120.3 48.4 %copy-start.10 = (bf16[256,256]{1,0:T(8,128)(2,1)S(1)}, bf16[256,256]{1,0:T(8,128)(2,1)}, u32[]{:S(2)}) copy-start(bf16[256,256]{1,0:T(8,128)(2,1)} %param.21) | copy-start | bytes 393220
  120.3 55.7 %copy-start.11 = (bf16[256,256]{1,0:T(8,128)(2,1)S(1)}, bf16[256,256]{1,0:T(8,128)(2,1)}, u32[]{:S(2)}) copy-start(bf16[256,256]{1,0:T(8,128)(2,1)} %param.23) | copy-start | bytes 393220
  120.3 63.7 %all-to-all-start = ((bf16[64,4,4,6,130]{4,0,3,2,1:T(8,128)(2,1)}), bf16[64,4,4,6,130]{4,0,3,2,1:T(8,128)(2,1)}, u32[]{:S(2)}, u32[]{:S(2)}) async-start(bf16[64,4,4,6,130]{4,0,3,2,1:T(8,128)(2,1)} %pad_maximum_fusion), calls=%async_computation | async-start | bytes 6291456 | tf_op jit(solution)/shard_map/all_to_all | solution.py:138
  125.1 58.9 %copy-start.12 = (s32[16,4,128]{2,1,0:T(4,128)S(1)}, s32[16,4,128]{2,1,0:T(4,128)}, u32[]{:S(2)}) copy-start(s32[16,4,128]{2,1,0:T(4,128)} %param.27) | copy-start | bytes 98308
  125.1 131.5 %all-gather.6.cloned.1.call-start = ((), (), s32[]{:S(2)}) async-start(), calls=%async_computation.3 | async-start | bytes 1310720 | tf_op jit(solution)/shard_map/all_gather | solution.py:122
  196.4 1.9 copy-start.2
  196.4 2.1 copy-start.9
  251.8 39.8 %all-to-all-start.1 = ((f32[256,1,4,4,128]{4,3,2,1,0:T(4,128)}), f32[256,1,4,4,128]{4,3,2,1,0:T(4,128)}, u32[]{:S(2)}, u32[]{:S(2)}) async-start(f32[256,1,4,4,128]{4,3,2,1,0:T(4,128)} %bitcast.218), calls=%async_computation.1 | async-start | bytes 4194304 | tf_op jit(solution)/shard_map/all_to_all | solution.py:157
  287.9 6.1 %copy-start.4 = (bf16[64,16,4,128]{3,2,1,0:T(4,128)(2,1)S(1)}, bf16[64,16,4,128]{3,2,1,0:T(4,128)(2,1)}, u32[]{:S(2)}) copy-start(bf16[64,16,4,128]{3,2,1,0:T(4,128)(2,1)} %param.15) | copy-start | bytes 3145732
  291.6 2.3 copy-start.8
  291.6 4.7 %copy-start.1 = (bf16[2048,384]{1,0:T(8,128)(2,1)S(1)}, bf16[2048,384]{1,0:T(8,128)(2,1)}, u32[]{:S(2)}) copy-start(bf16[2048,384]{1,0:T(8,128)(2,1)} %param.16) | copy-start | bytes 4718596
Sparse Core Ops, SparseCore 0:
  52.7 19.5 all-gather.3
  127.5 27.7 all-gather.5
where the time goes:
time: 305 us; the launch traced here: 303 us
  local copies, waits for them, and re-layouts  140 us (46%)
  blocking collectives  55.6 us (18%)
  matrix products  35.6 us (12%)
  other arithmetic  22.6 us (7%)
  waiting for transfers between devices  17.9 us (6%)
  starting transfers between devices  16.8 us (6%)
  between operations  14.4 us (5%)
    unnamed x1, blocking collectives  35.2 us
    gather x2, local copies, waits for them, and re-layouts, on_device(): values = jnp.take(piece, jnp.clip(targets, 0, piece.shape[1] - 1), axis=1)  33 us
    dot_general x1, matrix products, on_device(): jnp.einsum('csij,ch->hsij', normed, full_in, preferred_element_type=jnp.f...  20.7 us
    gather x2, local copies, waits for them, and re-layouts, pad_blocks(): jnp.take(strips, slot_index.reshape(-1), axis=1)  19.6 us
    unnamed x54, local copies, waits for them, and re-layouts  15.9 us
    ppermute x1, waiting for transfers between devices, padded_2(): lax.ppermute(tail, axis, [(i, (i + 1) % count) for i in range(ends)])  12.9 us
    all_gather x1, blocking collectives, on_device(): lax.all_gather(out_weight, ('chan', 'sec'), axis=0, tiled=True)  7.95 us
    select_n x1, other arithmetic, pad_blocks(): picked = jnp.where(valid[None, :, :, None], picked, jnp.zeros_like(picked))  7.94 us
  transfers between devices with their start and end apart: 6, of which 2 were waited for; matrix products, arithmetic and copies ran while one was open for 51% of the time, Pallas kernels for 0%

commit v1 on v0

--- a/solution.py
+++ b/solution.py
@@ -154,9 +154,18 @@
     summed, _ = lax.scan(
         add_group, jnp.zeros((channels,) + hidden.shape[1:], jnp.float32), (hid_groups, out_groups)
     )
-    update = lax.all_to_all(
-        summed[:, None], ("chan", "sec"), split_axis=0, concat_axis=1, tiled=True
-    )
+    x = summed[:, None]
+    ways, here = (lax.axis_size(("chan", "sec")), lax.axis_index(("chan", "sec")))
+    width_2 = x.shape[0] // ways
+    turned = jnp.roll(x, -here * width_2, axis=0)
+    got = [lax.slice_in_dim(turned, 0, width_2, axis=0)]
+    for far in range(1, ways):
+        sent = lax.slice_in_dim(turned, far * width_2, (far + 1) * width_2, axis=0)
+        got.append(
+            lax.ppermute(sent, ("chan", "sec"), [(d, (d + far) % ways) for d in range(ways)])
+        )
+    line = jnp.concatenate(got[::-1], axis=1)
+    update = jnp.roll(line, (here + 1) * got[0].shape[1], axis=1)
     update = update.reshape(chan_local, slot_count, block_rows, block_cols)
     total = (
         ocean_state.astype(jnp.float32)

time: 305 us -> 316 us (1.036)
  local copies, waits for them, and re-layouts: 140 us -> 150 us
    unnamed x54 -> x59, local copies, waits for them, and re-layouts: 15.9 us -> 23.5 us
    all_to_all x1 -> x0, starting transfers between devices: 4.7 us -> none  [on_device(): lax.all_to_all(summed[:, None], ('chan', 'sec'), split_axis=0, concat_axi...]
  transfers between devices with their start and end apart: 6 -> 8, of which waited for: 2 -> 2; matrix products, arithmetic and copies ran while one was open for 51% -> 51% of each run, Pallas kernels for 0% -> 0%
where the time goes in v1:
time: 316 us; the launch traced here: 313 us
  local copies, waits for them, and re-layouts  150 us (47%)
  blocking collectives  55.6 us (18%)
  matrix products  36.9 us (12%)
  other arithmetic  23.8 us (8%)
  waiting for transfers between devices  17.7 us (6%)
  between operations  14.6 us (5%)
  starting transfers between devices  14.1 us (4%)
    unnamed x1, blocking collectives  35.2 us
    gather x2, local copies, waits for them, and re-layouts, on_device(): values = jnp.take(piece, jnp.clip(targets, 0, piece.shape[1] - 1), axis=1)  32.7 us
    unnamed x59, local copies, waits for them, and re-layouts  23.5 us
    dot_general x1, matrix products, on_device(): jnp.einsum('csij,ch->hsij', normed, full_in, preferred_element_type=jnp.f...  20.8 us
    gather x2, local copies, waits for them, and re-layouts, pad_blocks(): jnp.take(strips, slot_index.reshape(-1), axis=1)  19.5 us
    ppermute x1, waiting for transfers between devices, padded_2(): lax.ppermute(tail, axis, [(i, (i + 1) % count) for i in range(ends)])  12.5 us
    all_gather x1, blocking collectives, on_device(): lax.all_gather(out_weight, ('chan', 'sec'), axis=0, tiled=True)  7.95 us
    select_n x1, other arithmetic, pad_blocks(): picked = jnp.where(valid[None, :, :, None], picked, jnp.zeros_like(picked))  7.94 us
  transfers between devices with their start and end apart: 8, of which 2 were waited for; matrix products, arithmetic and copies ran while one was open for 51% of the time, Pallas kernels for 0%

profile of v1, /device:TPU:0, one launch (start us, length us, event | category | flops | bytes accessed | tf_op | source)
XLA Modules:
  0.0 313.1 jit_solution(11479914184458584081)
XLA Ops:
  6.5 3.6 %fusion.53 = (bf16[64,16,1,128]{3,2,1,0:T(2,128)(2,1)S(1)}, bf16[64,16,1,128]{3,2,1,0:T(2,128)(2,1)}) fusion(bf16[64,16,4,128]{3,2,1,0:T(4,128)(2,1)} %param.15), kind=kLoop, calls=%fused_computation.107 | loop fusion | bytes 1048576 | tf_op jit(solution)/shard_map/slice | solution.py:30
  10.2 5.7 %fusion.51 = (bf16[64,16,1,1]{3,2,1,0:T(2,128)(2,1)}, bf16[64,16,1,1]{3,2,1,0:T(2,128)(2,1)}, bf16[64,16,1,1]{3,2,1,0:T(2,128)(2,1)}, bf16[64,16,1,1]{3,2,1,0:T(2,128)(2,1)}) fusion(bf16[64,16,4,128]{3,2,1,0:T(4,128)(2,1)} %param.15), kind=kLoop, calls=%fused_computation.105 | loop fusion | bytes 16384 | tf_op jit(solution)/shard_map/slice | solution.py:36
  15.8 2.3 fusion.52
  27.0 7.9 %copy.135 = bf16[64,16,4,1]{2,0,1,3:T(8,128)(2,1)} copy(bf16[64,16,4,1]{3,2,1,0:T(4,128)(2,1)} %get-tuple-element.83) | data formatting | bytes 16384 | tf_op jit(solution)/shard_map/squeeze | solution.py:31
  34.9 7.9 %copy.136 = bf16[64,16,4,1]{2,0,1,3:T(8,128)(2,1)} copy(bf16[64,16,4,1]{3,2,1,0:T(4,128)(2,1)} %get-tuple-element.82) | data formatting | bytes 16384 | tf_op jit(solution)/shard_map/squeeze | solution.py:32
  42.8 2.2 copy_bitcast_fusion
  44.9 3.3 %concatenate.50 = bf16[64,16,268]{2,0,1:T(8,128)(2,1)S(1)} concatenate(bf16[64,16,128]{2,0,1:T(8,128)(2,1)} %get-tuple-element.92, bf16[64,16,128]{2,0,1:T(8,128)(2,1)} %get-tuple-element.91, bf16[64,16,4]{2,0,1:T(8,128)(2,1)} %bitcast.220, bf16[64,16,4]{2,0,1:T(8,128)(2,1)} %bitcast.221, bf16[64,16,1]{2,0,1:T(8,128)(2,1)} %copy.73, bf16[64,16,1]{2,0,1:T(8,128)(2,1)} %copy.74, ...), dimensions={2} | concatenate | bytes 1097728 | tf_op jit(solution)/shard_map/concatenate | solution.py:27
  48.3 5.8 %collective-permute-start = (bf16[64,16,268]{2,0,1:T(8,128)(2,1)S(1)}, bf16[64,16,268]{2,0,1:T(8,128)(2,1)}, u32[]{:S(2)}, u32[]{:S(2)}) collective-permute-start(bf16[64,16,268]{2,0,1:T(8,128)(2,1)S(1)} %concatenate.50), channel_id=1, source_target_pairs={{0,4},{4,8},{8,12},{1,5},{5,9},{9,13},{2,6},{6,10},{10,14},{3,7},{... | collective-permute-start | bytes 1646600 | tf_op jit(solution)/shard_map/ppermute | solution.py:17
  54.1 1.5 collective-permute-start.1
  55.6 1.7 copy.82
  57.5 12.5 %collective-permute-done = bf16[64,16,268]{2,0,1:T(8,128)(2,1)} collective-permute-done((bf16[64,16,268]{2,0,1:T(8,128)(2,1)S(1)}, bf16[64,16,268]{2,0,1:T(8,128)(2,1)}, u32[]{:S(2)}, u32[]{:S(2)}) %collective-permute-start) | collective-permute-done | bytes 548896 | tf_op jit(solution)/shard_map/ppermute | solution.py:17
  70.0 5.1 %collective-permute-done.1 = bf16[64,16,268]{2,0,1:T(8,128)(2,1)} collective-permute-done((bf16[64,16,268]{2,0,1:T(8,128)(2,1)S(1)}, bf16[64,16,268]{2,0,1:T(8,128)(2,1)}, u32[]{:S(2)}, u32[]{:S(2)}) %collective-permute-start.1) | collective-permute-done | bytes 548896 | tf_op jit(solution)/shard_map/ppermute | solution.py:19
  75.1 3.3 %pad_maximum_fusion.1 = bf16[64,48,268]{2,0,1:T(8,128)(2,1)} fusion(bf16[64,16,268]{2,0,1:T(8,128)(2,1)} %collective-permute-done.1, bf16[64,16,268]{2,0,1:T(8,128)(2,1)S(1)} %concatenate.50, bf16[64,16,268]{2,0,1:T(8,128)(2,1)} %collective-permute-done), kind=kLoop, calls=%fused_computation.37 | loop fusion | flops 1646592 | bytes 3293184 | tf_op jit(solution)/shard_map/concatenate | solution.py:15
  78.4 5.8 %gather_fusion = bf16[128,64,268]{2,1,0:T(8,128)(2,1)} fusion(bf16[64,48,268]{2,0,1:T(8,128)(2,1)} %pad_maximum_fusion.1, s32[1024]{0:T(1024)S(1)} %pad_clamp_fusion), kind=kCustom, calls=%fused_computation | custom fusion | bytes 8782336 | tf_op jit(solution)/shard_map/jit(_take)/gather | solution.py:45
  84.1 13.8 %copy.78 = bf16[64,16,8,268]{0,1,3,2:T(8,128)(2,1)} copy(bf16[64,16,8,268]{3,0,2,1:T(8,128)(2,1)} %bitcast.213) | data formatting | bytes 8781824 | tf_op jit(solution)/shard_map/jit(_take)/gather | solution.py:45
  97.9 7.9 %select_select_fusion = bf16[64,16,8,268]{0,1,3,2:T(8,128)(2,1)} fusion(bf16[64,16,8,268]{0,1,3,2:T(8,128)(2,1)} %copy.78, pred[16,8]{0,1:T(8,128)(4,1)S(1)} %get-tuple-element.65, pred[16,8]{0,1:T(8,128)(4,1)S(1)} %get-tuple-element.88), kind=kLoop, calls=%fused_computation.10 | loop fusion | flops 4390912 | bytes 8782080 | tf_op jit(solution)/shard_map/jit(_where)/select_n | solution.py:48
  108.4 2.3 fusion.48
  110.6 1.5 copy.79
  115.8 1.5 copy.83
  117.3 1.4 copy.84
  118.7 1.3 maximum_bitcast_fusion
  120.1 1.4 maximum_bitcast_fusion.1
  121.5 4.2 %pad_maximum_fusion = bf16[64,4,4,6,130]{4,0,3,2,1:T(8,128)(2,1)} fusion(bf16[64,4,4,1,130]{4,0,3,2,1:T(8,128)(2,1)S(1)} %maximum_bitcast_fusion.1, bf16[64,4,4,4,1]{4,0,3,2,1:T(8,128)(2,1)} %copy.84, bf16[64,4,4,4,128]{4,0,3,2,1:T(8,128)(2,1)S(1)} %bitcast.216, bf16[64,4,4,4,1]{4,0,3,2,1:T(8,128)(2,1)} %copy.83, ...), kind=kLoop, calls=%fused_computation.36 | loop fusion | flops 7987200 | bytes 3194880 | tf_op jit(solution)/shard_map/concatenate | solution.py:71
  125.8 4.8 %all-to-all-start = ((bf16[64,4,4,6,130]{4,0,3,2,1:T(8,128)(2,1)}), bf16[64,4,4,6,130]{4,0,3,2,1:T(8,128)(2,1)}, u32[]{:S(2)}, u32[]{:S(2)}) async-start(bf16[64,4,4,6,130]{4,0,3,2,1:T(8,128)(2,1)} %pad_maximum_fusion), calls=%async_computation | async-start | bytes 6291456 | tf_op jit(solution)/shard_map/all_to_all | solution.py:138
  130.6 1.3 convolution_convert_fusion.1
  133.7 35.2 %all-reduce.2 = (bf16[256]{0:T(256)(128)(2,1)S(1)}, bf16[256]{0:T(256)(128)(2,1)S(1)}) all-reduce(bf16[256]{0:T(256)(128)(2,1)S(1)} %dynamic-update-slice, bf16[256]{0:T(256)(128)(2,1)S(1)} %dynamic-update-slice.1), channel_id=1, replica_groups=mesh['ens'=2,'tile'=4,'chan'=2,'sec'=2] {'chan','sec'}, use_global_device_ids=true, to_apply=%add | all-reduce | flops 512 | bytes 2048
  169.0 5.1 %all-gather = bf16[4,1,256]{2,1,0:T(2,128)(2,1)S(1)} all-gather(bf16[1,1,256]{2,1,0:T(2,128)(2,1)S(1)} %reshape.158), channel_id=1, replica_groups=mesh['ens'=2,'tile'=4,'chan'=2,'sec'=2] {'chan','sec'}, dimensions={0}, use_global_device_ids=true | all-gather | bytes 2560 | tf_op jit(solution)/shard_map/all_gather | solution.py:131
  174.1 7.3 %all_gather.25 = bf16[256,1024]{1,0:T(8,128)(2,1)S(1)} all-gather(bf16[256,256]{1,0:T(8,128)(2,1)S(1)} %copy-done.9), channel_id=1, replica_groups=mesh['ens'=2,'tile'=4,'chan'=2,'sec'=2] {'chan','sec'}, dimensions={1}, use_global_device_ids=true | all-gather | bytes 655360 | tf_op jit(solution)/shard_map/all_gather | solution.py:130
  181.4 7.9 %all_gather.21 = bf16[1024,256]{1,0:T(8,128)(2,1)} all-gather(bf16[256,256]{1,0:T(8,128)(2,1)S(1)} %copy-done.10), channel_id=1, replica_groups=mesh['ens'=2,'tile'=4,'chan'=2,'sec'=2] {'chan','sec'}, dimensions={0}, use_global_device_ids=true | all-gather | bytes 655360 | tf_op jit(solution)/shard_map/all_gather | solution.py:132
  189.4 7.3 %copy.90 = bf16[4,64,1,4,6,130]{1,0,5,4,3,2:T(4,128)(2,1)} copy(bf16[4,64,1,4,6,130]{5,1,4,3,0,2:T(8,128)(2,1)} %bitcast.24) | data formatting | bytes 3194880 | tf_op jit(solution)/shard_map/all_to_all | solution.py:138
  196.7 5.1 %squeeze.76 = bf16[256,4,6,130]{0,3,2,1:T(8,128)(2,1)} reshape(bf16[4,64,1,4,6,130]{1,0,5,4,3,2:T(4,128)(2,1)} %copy.90) | data formatting | bytes 3194880 | tf_op jit(solution)/shard_map/squeeze | solution.py:138
  201.7 1.8 fusion.29
  203.6 1.7 fusion.31
  209.5 20.8 %fusion.7 = bf16[1024,4,4,128]{0,3,2,1:T(8,128)(2,1)} fusion(f32[1024]{0:T(1024)S(1)} %bitcast.234, f32[4,4,128,256]{3,2,1,0:T(8,128)S(1)} %get-tuple-element.90, f32[256]{0:T(256)S(1)} %convert_element_type.43, f32[4,4,128]{2,1,0:T(4,128)S(1)} %add_rsqrt_fusion, bf16[256,1024]{1,0:T(8,128)(2,1)S(1)} %all_gather.25), kind=kOutput, calls=%fused_computation.13 | convolution fusion | flops 1213726720 | bytes 6829056 | tf_op jit(solution)/shard_map/csij,ch->hsij/dot_general | solution.py:149
  230.3 7.9 %reshape.134 = bf16[4,256,4,4,128]{1,0,4,3,2:T(4,128)(2,1)} reshape(bf16[1024,4,4,128]{0,3,2,1:T(8,128)(2,1)} %fusion.7) | data formatting | bytes 8388608 | tf_op jit(solution)/shard_map/reshape | solution.py:153
  238.2 7.5 %copy.101 = bf16[4,256,4,4,128]{4,1,3,2,0:T(8,128)(2,1)} copy(bf16[4,256,4,4,128]{1,0,4,3,2:T(4,128)(2,1)} %reshape.134) | data formatting | bytes 8388608
  245.7 9.9 %while.11 = (s32[]{:T(128)}, f32[256,4,4,128]{3,0,2,1:T(8,128)S(1)}, bf16[4,256,256]{2,1,0:T(8,128)(2,1)}, bf16[4,256,4,4,128]{4,1,3,2,0:T(8,128)(2,1)}, s32[]{:T(128)}, /*index=5*/s32[]{:T(128)}) while((s32[]{:T(128)}, f32[256,4,4,128]{3,0,2,1:T(8,128)S(1)}, bf16[4,256,256]{2,1,0:T(8,128)(2,1)}, ...), condition=%wide.region_2.3_spmd.clone, body=%wide.region_1.2_spmd.clone.sunk | while | flops 270532608 | bytes 7472207 | solution.py:154
  245.7 1.8 convolution_convert_fusion.3
  248.1 1.8 convolution_convert_fusion.3
  250.6 1.8 convolution_convert_fusion.3
  253.1 1.8 convolution_convert_fusion.3
  256.0 1.3 copy-done.5
  258.5 1.6 collective-permute-start.2
  260.8 2.0 copy.103
  262.8 29.4 %gather_fusion.1 = bf16[8192,64]{1,0:T(8,128)(2,1)} fusion(bf16[64,8192]{0,1:T(8,128)(2,1)S(1)} %copy.103, s32[8192]{0:T(1024)S(1)} %broadcast_clamp_fusion), kind=kCustom, calls=%fused_computation.1 | custom fusion | bytes 2129920 | tf_op jit(solution)/shard_map/jit(_take)/gather | solution.py:124
  292.2 3.3 %copy.104 = bf16[64,16,4,128]{3,2,1,0:T(4,128)(2,1)S(1)} copy(bf16[64,16,4,128]{0,3,2,1:T(8,128)(2,1)} %bitcast.215) | data formatting | bytes 2097152 | tf_op jit(solution)/shard_map/jit(_take)/gather | solution.py:124
  302.5 1.4 copy.102
  303.8 2.4 multiply_convert_fusion.1
  (110 shorter events, 32.5 us)
Async XLA Ops:
  6.5 124.1 %copy-start = (bf16[2048,384]{1,0:T(8,128)(2,1)S(1)}, bf16[2048,384]{1,0:T(8,128)(2,1)}, u32[]{:S(2)}) copy-start(bf16[2048,384]{1,0:T(8,128)(2,1)} %param.16) | copy-start | bytes 4718596
  6.5 9.3 %copy-start.3 = (bf16[64,16,4,128]{3,2,1,0:T(4,128)(2,1)S(1)}, bf16[64,16,4,128]{3,2,1,0:T(4,128)(2,1)}, u32[]{:S(2)}) copy-start(bf16[64,16,4,128]{3,2,1,0:T(4,128)(2,1)} %param.15) | copy-start | bytes 3145732
  6.5 195.2 %all-gather.4.cloned.1.call-start = ((), (), s32[]{:S(2)}) async-start(), calls=%async_computation.1 | async-start | bytes 1474560 | tf_op jit(solution)/shard_map/all_gather | solution.py:127
  34.9 22.4 %copy-start.14 = (s32[16,8]{0,1:T(8,128)S(1)}, s32[16,8]{0,1:T(8,128)}, u32[]{:S(2)}) copy-start(s32[16,8]{0,1:T(8,128)} %param.26) | copy-start | bytes 1540
  48.3 21.7 %collective-permute-start = (bf16[64,16,268]{2,0,1:T(8,128)(2,1)S(1)}, bf16[64,16,268]{2,0,1:T(8,128)(2,1)}, u32[]{:S(2)}, u32[]{:S(2)}) collective-permute-start(bf16[64,16,268]{2,0,1:T(8,128)(2,1)S(1)} %concatenate.50), channel_id=1, source_target_pairs={{0,4},{4,8},{8,12},{1,5},{5,9},{9,13},{2,6},{6,10},{10,14},{3,7},{... | collective-permute-start | bytes 1646600 | tf_op jit(solution)/shard_map/ppermute | solution.py:17
  54.1 21.0 %collective-permute-start.1 = (bf16[64,16,268]{2,0,1:T(8,128)(2,1)S(1)}, bf16[64,16,268]{2,0,1:T(8,128)(2,1)}, u32[]{:S(2)}, u32[]{:S(2)}) collective-permute-start(bf16[64,16,268]{2,0,1:T(8,128)(2,1)S(1)} %concatenate.50), channel_id=1, source_target_pairs={{4,0},{8,4},{12,8},{5,1},{9,5},{13,9},{6,2},{10,6},{14,10},{7,3},{... | collective-permute-start | bytes 1646600 | tf_op jit(solution)/shard_map/ppermute | solution.py:19
  108.4 13.1 %copy-start.7 = (bf16[64,16,4,128]{3,0,2,1:T(8,128)(2,1)S(1)}, bf16[64,16,4,128]{3,0,2,1:T(8,128)(2,1)}, u32[]{:S(2)}) copy-start(bf16[64,16,4,128]{3,0,2,1:T(8,128)(2,1)} %copy.82) | copy-start | bytes 3145732
  125.7 4.9 %copy-start.12 = (bf16[384,64]{0,1:T(8,128)(2,1)S(1)}, bf16[384,64]{0,1:T(8,128)(2,1)}, u32[]{:S(2)}) copy-start(bf16[384,64]{0,1:T(8,128)(2,1)} %param.17) | copy-start | bytes 147460
  125.7 6.3 %copy-start.19 = (u32[32]{0:T(128)S(1)}, u32[32]{0:T(128)}, u32[]{:S(2)}) copy-start(u32[32]{0:T(128)} %constant.178) | copy-start | bytes 388
  125.7 7.5 %copy-start.15 = (bf16[64]{0:T(256)(128)(2,1)S(1)}, bf16[64]{0:T(256)(128)(2,1)}, u32[]{:S(2)}) copy-start(bf16[64]{0:T(256)(128)(2,1)} %param.19) | copy-start | bytes 388
  125.7 7.8 %copy-start.16 = (bf16[64]{0:T(256)(128)(2,1)S(1)}, bf16[64]{0:T(256)(128)(2,1)}, u32[]{:S(2)}) copy-start(bf16[64]{0:T(256)(128)(2,1)} %param.20) | copy-start | bytes 388
  125.7 43.3 %copy-start.17 = (bf16[256]{0:T(256)(128)(2,1)S(1)}, bf16[256]{0:T(256)(128)(2,1)}, u32[]{:S(2)}) copy-start(bf16[256]{0:T(256)(128)(2,1)} %param.22) | copy-start | bytes 1540
  125.7 48.4 %copy-start.9 = (bf16[256,256]{1,0:T(8,128)(2,1)S(1)}, bf16[256,256]{1,0:T(8,128)(2,1)}, u32[]{:S(2)}) copy-start(bf16[256,256]{1,0:T(8,128)(2,1)} %param.21) | copy-start | bytes 393220
  125.7 55.7 %copy-start.10 = (bf16[256,256]{1,0:T(8,128)(2,1)S(1)}, bf16[256,256]{1,0:T(8,128)(2,1)}, u32[]{:S(2)}) copy-start(bf16[256,256]{1,0:T(8,128)(2,1)} %param.23) | copy-start | bytes 393220
  125.8 63.6 %copy-start.11 = (s32[16,4,128]{2,1,0:T(4,128)S(1)}, s32[16,4,128]{2,1,0:T(4,128)}, u32[]{:S(2)}) copy-start(s32[16,4,128]{2,1,0:T(4,128)} %param.27) | copy-start | bytes 98308
  125.8 63.6 %all-to-all-start = ((bf16[64,4,4,6,130]{4,0,3,2,1:T(8,128)(2,1)}), bf16[64,4,4,6,130]{4,0,3,2,1:T(8,128)(2,1)}, u32[]{:S(2)}, u32[]{:S(2)}) async-start(bf16[64,4,4,6,130]{4,0,3,2,1:T(8,128)(2,1)} %pad_maximum_fusion), calls=%async_computation | async-start | bytes 6291456 | tf_op jit(solution)/shard_map/all_to_all | solution.py:138
  130.5 130.2 %all-gather.6.cloned.1.call-start = ((), (), s32[]{:S(2)}) async-start(), calls=%async_computation.2 | async-start | bytes 1310720 | tf_op jit(solution)/shard_map/all_gather | solution.py:122
  201.7 3.6 %copy-start.2 = (bf16[256,4,6,130]{0,3,2,1:T(8,128)(2,1)S(1)}, bf16[256,4,6,130]{0,3,2,1:T(8,128)(2,1)}, u32[]{:S(2)}) copy-start(bf16[256,4,6,130]{0,3,2,1:T(8,128)(2,1)} %squeeze.76) | copy-start | bytes 4792324
  201.7 3.6 %copy-start.8 = (bf16[9,256,256]{1,2,0:T(8,128)(2,1)S(1)}, bf16[9,256,256]{1,2,0:T(8,128)(2,1)}, u32[]{:S(2)}) copy-start(bf16[9,256,256]{1,2,0:T(8,128)(2,1)} %all-gather.4.cloned.1.call-done) | copy-start | bytes 3538948
  255.5 5.1 %copy-start.13 = (s32[16,4,128]{2,1,0:T(4,128)S(1)}, s32[16,4,128]{2,1,0:T(4,128)}, u32[]{:S(2)}) copy-start(s32[16,4,128]{2,1,0:T(4,128)} %param.25) | copy-start | bytes 98308
  255.6 5.1 %copy-start.18 = (bf16[64]{0:T(256)(128)(2,1)S(1)}, bf16[64]{0:T(256)(128)(2,1)}, u32[]{:S(2)}) copy-start(bf16[64]{0:T(256)(128)(2,1)} %param.24) | copy-start | bytes 388
  256.0 1.4 copy-start.5
  258.5 37.0 %collective-permute-start.2 = (f32[64,1,4,4,128]{4,0,3,2,1:T(8,128)}, f32[64,1,4,4,128]{4,0,3,2,1:T(8,128)}, u32[]{:S(2)}, u32[]{:S(2)}) collective-permute-start(f32[64,1,4,4,128]{4,0,3,2,1:T(8,128)} %get-tuple-element.77), channel_id=1, source_target_pairs={{0,3},{1,0},{2,1},{3,2},{4,7},{5,4},{6,5},{7,6},{8,11},{9,8},{10,9... | collective-permute-start | bytes 1572872 | tf_op jit(solution)/shard_map/ppermute | solution.py:165
  260.1 36.5 %collective-permute-start.3 = (f32[64,1,4,4,128]{4,0,3,2,1:T(8,128)}, f32[64,1,4,4,128]{4,0,3,2,1:T(8,128)}, u32[]{:S(2)}, u32[]{:S(2)}) collective-permute-start(f32[64,1,4,4,128]{4,0,3,2,1:T(8,128)} %get-tuple-element.76), channel_id=1, source_target_pairs={{0,2},{1,3},{2,0},{3,1},{4,6},{5,7},{6,4},{7,5},{8,10},{9,11},{10,... | collective-permute-start | bytes 1572872 | tf_op jit(solution)/shard_map/ppermute | solution.py:165
  260.6 37.1 %collective-permute-start.4 = (f32[64,1,4,4,128]{4,0,3,2,1:T(8,128)}, f32[64,1,4,4,128]{4,0,3,2,1:T(8,128)}, u32[]{:S(2)}, u32[]{:S(2)}) collective-permute-start(f32[64,1,4,4,128]{4,0,3,2,1:T(8,128)} %get-tuple-element.75), channel_id=1, source_target_pairs={{0,1},{1,2},{2,3},{3,0},{4,5},{5,6},{6,7},{7,4},{8,9},{9,10},{10,1... | collective-permute-start | bytes 1572872 | tf_op jit(solution)/shard_map/ppermute | solution.py:165
  292.2 6.6 %copy-start.6 = (f32[256,1,4,4,128]{4,0,3,2,1:T(8,128)S(1)}, f32[256,1,4,4,128]{4,0,3,2,1:T(8,128)}, u32[]{:S(2)}) copy-start(f32[256,1,4,4,128]{4,0,3,2,1:T(8,128)} %copy-done.5) | copy-start | bytes 6291460
  302.2 1.6 copy-start.4
  302.2 4.0 %copy-start.1 = (bf16[2048,384]{1,0:T(8,128)(2,1)S(1)}, bf16[2048,384]{1,0:T(8,128)(2,1)}, u32[]{:S(2)}) copy-start(bf16[2048,384]{1,0:T(8,128)(2,1)} %param.16) | copy-start | bytes 4718596
Sparse Core Ops, SparseCore 0:
  55.7 19.6 all-gather.3
  133.0 27.7 all-gather.5
